TPU v7x, 32 devices: a whole 2x2x4 slice. The times are simulated.
32 devices in a mesh: outer: 16 (over z, y, core), inner: 2 (over x).
Axes of the slice: x: 2, y: 2, z: 4, core: 2. Of those that a mesh axis runs over, the one named last changes fastest.
Arguments:
- layer_input: bfloat16 [4096, 8192], P(('outer', 'inner')), may hold values from -6 to 6
- queries: bfloat16 [4096, 4096], P(('outer', 'inner')), may hold values from -8 to 8
- key_states: bfloat16 [4096, 512], P(('outer', 'inner')), may hold values from -8 to 8
- output_grad: bfloat16 [4096, 4096], P(('outer', 'inner')), may hold values from -24 to 24
- value_weight: bfloat16 [8192, 512], P('inner'), may hold values from -0.0625 to 0.0625
- value_scales: float32 [8192, 2], P('inner'), may hold values from 0.5 to 2
Outputs:
- query_grad: bfloat16 [4096, 4096], P(('outer', 'inner'))
- key_grad: bfloat16 [4096, 512], P(('outer', 'inner'))
- weight_grad: float32 [8192, 512], P(('outer', 'inner'))
All inputs are finite; a program needn't handle non-finite values.
Results may differ from a plain program's by a relative error of at most 0.034.
Values may be sent and summed in bfloat16 or wider, within the bound.
A program may use at most 192 MiB of HBM per device.

v0:
```python
import jax
import jax.numpy as jnp
from jax import lax
from jax.sharding import PartitionSpec as P

KV_HEADS = 4
HEAD_DIM = 128
QUANT_BLOCK = 256
GROUP_SIZE = 8


clip_ratio = 1.5


def dequantize(quant_values, quant_scales):
    leading = quant_values.shape[:-1]
    blocks = quant_values.astype(jnp.float32).reshape(leading + (quant_scales.shape[-1], -1))
    return (blocks * quant_scales[..., None]).reshape(leading + (-1,))


def quantize(gradient):
    leading = gradient.shape[:-1]
    blocks = gradient.reshape(leading + (-1, QUANT_BLOCK))
    block_scale = clip_ratio * jnp.sqrt(jnp.mean(blocks * blocks, axis=-1) + 1e-06)
    scaled = jnp.clip(blocks / block_scale[..., None], -1.0, 1.0)
    quant = scaled.astype(jnp.bfloat16).reshape(gradient.shape)
    return (quant, block_scale)


def attend_backward(queries, key_states, value_rows, output_grad):
    count = queries.shape[0]
    query_heads = queries.reshape(count, KV_HEADS, GROUP_SIZE, HEAD_DIM)
    key_heads = key_states.reshape(count, KV_HEADS, HEAD_DIM)
    value_heads = value_rows.reshape(count, KV_HEADS, HEAD_DIM)
    grad_heads = output_grad.reshape(count, KV_HEADS, GROUP_SIZE, HEAD_DIM)
    score_scale = HEAD_DIM ** (-0.5)
    scores = score_scale * jnp.einsum(
        "tgek,sgk->gets", query_heads, key_heads, preferred_element_type=jnp.float32
    )
    position = jnp.arange(count)
    causal = position[:, None] >= position[None, :]
    scores = jnp.where(causal, scores, -jnp.inf)
    row_peak = jnp.max(scores, axis=-1, keepdims=True)
    exp_scores = jnp.exp(scores - row_peak)
    probs = exp_scores / jnp.sum(exp_scores, axis=-1, keepdims=True)
    probs_low = probs.astype(jnp.bfloat16)
    value_grad = jnp.einsum(
        "gets,tgek->sgk", probs_low, grad_heads, preferred_element_type=jnp.float32
    ).astype(jnp.bfloat16)
    prob_grad = jnp.einsum(
        "tgek,sgk->gets", grad_heads, value_heads, preferred_element_type=jnp.float32
    )
    row_delta = jnp.sum(probs * prob_grad, axis=-1, keepdims=True)
    score_grad = (probs * (prob_grad - row_delta)).astype(jnp.bfloat16)
    query_grad = (
        score_scale
        * jnp.einsum("gets,sgk->tgek", score_grad, key_heads, preferred_element_type=jnp.float32)
    ).astype(jnp.bfloat16)
    key_grad = (
        score_scale
        * jnp.einsum("gets,tgek->sgk", score_grad, query_heads, preferred_element_type=jnp.float32)
    ).astype(jnp.bfloat16)
    return (
        query_grad.reshape(count, -1),
        key_grad.reshape(count, -1),
        value_grad.reshape(count, -1),
    )


def on_device(layer_input, queries, key_states, output_grad, value_weight, value_scales):
    pieces = (
        lax.all_gather(value_weight, "inner", axis=0, tiled=True),
        lax.all_gather(value_scales.astype(jnp.bfloat16), "inner", axis=0, tiled=True).astype(
            jnp.float32
        ),
    )
    weight_rows = dequantize(pieces[0], pieces[1]).astype(jnp.bfloat16)
    value_sum = jnp.dot(layer_input, weight_rows, preferred_element_type=jnp.float32)
    value_rows = value_sum.astype(jnp.bfloat16)
    query_grad, key_grad, value_grad = attend_backward(queries, key_states, value_rows, output_grad)
    outer_count = lax.axis_size("outer")
    inner_count = lax.axis_size("inner")
    owner_count = layer_input.shape[1] // (outer_count * inner_count)
    gradient = jnp.einsum("td,tk->dk", layer_input, value_grad, preferred_element_type=jnp.float32)
    quant, block_scale = quantize(gradient)
    quant_grid = quant.reshape(outer_count, inner_count, owner_count, -1)
    scale_grid = block_scale.reshape(outer_count, inner_count, owner_count, -1)
    pieces = (
        lax.all_to_all(quant_grid, "outer", split_axis=0, concat_axis=0, tiled=True),
        lax.all_to_all(
            scale_grid.astype(jnp.bfloat16), "outer", split_axis=0, concat_axis=0, tiled=True
        ).astype(scale_grid.dtype),
    )
    partial_sums = jnp.sum(dequantize(pieces[0], pieces[1]), axis=0)
    owned_rows = lax.psum_scatter(
        partial_sums.astype(jnp.bfloat16), "inner", scatter_dimension=0, tiled=True
    ).astype(jnp.float32)
    return (query_grad, key_grad, owned_rows.reshape(owner_count, -1))


def solution(mesh):
    in_specs = (
        P(("outer", "inner"), None),
        P(("outer", "inner"), None),
        P(("outer", "inner"), None),
        P(("outer", "inner"), None),
        P("inner", None),
        P("inner", None),
    )
    out_specs = (
        P(("outer", "inner"), None),
        P(("outer", "inner"), None),
        P(("outer", "inner"), None),
    )
    return jax.shard_map(
        on_device, mesh=mesh, in_specs=in_specs, out_specs=out_specs, check_vma=False
    )
```

profile of v0, /device:TPU:10, one launch (start us, length us, event | category | flops | bytes accessed | tf_op | source)
XLA Modules:
  0.0 350.4 jit_solution(11030709793694477175)
XLA Ops:
  7.2 0.0 copy-start
  7.2 0.0 copy-start.3
  7.2 1.8 copy.92
  9.0 0.0 copy-done.3
  9.0 0.0 copy-start.1
  9.1 0.1 copy.79
  9.2 2.4 copy.93
  11.7 2.1 fusion.19
  13.8 0.0 copy-done.1
  13.8 2.3 fusion.8
  16.1 0.0 copy-done
  16.1 8.1 %bitcast_reduce_fusion = (f32[8192,2]{0,1:T(2,128)S(1)}, f32[8192,512]{0,1:T(8,128)}) fusion(bf16[128,512]{0,1:T(8,128)(2,1)S(1)} %bitcast.85, bf16[128,8192]{1,0:T(8,128)(2,1)S(1)} %copy-done), kind=kOutput, calls=%fused_computation.1 | convolution fusion | flops 1082114048 | bytes 19070976 | tf_op jit(solution)/shard_map/td,tk->dk/dot_general | solution.py:84
  24.2 0.1 fusion.18
  24.4 0.6 copy.71
  25.0 6.3 %all-to-all-start.1 = ((bf16[16,2,256,2]{2,1,3,0:T(2,128)(2,1)}), bf16[16,2,256,2]{2,1,3,0:T(2,128)(2,1)S(1)}, u32[]{:S(2)}, u32[]{:S(2)}) async-start(bf16[16,2,256,2]{2,1,3,0:T(2,128)(2,1)} %copy.71), calls=%async_computation.1 | async-start | bytes 65536 | tf_op jit(solution)/shard_map/all_to_all | solution.py:90
  31.3 2.6 copy.68
  33.9 12.0 %div.29 = f32[8192,2,256]{2,1,0:T(2,128)} broadcast(f32[8192,2]{1,0:T(8,128)} %copy.68), dimensions={0,1} | broadcast | bytes 16842752 | tf_op jit(solution)/shard_map/div | solution.py:25
  45.9 21.6 %div.30 = f32[16,2,256,512]{3,2,1,0:T(8,128)} reshape(f32[8192,2,256]{2,1,0:T(2,128)} %div.29) | data formatting | bytes 33554432 | tf_op jit(solution)/shard_map/div | solution.py:25
  67.5 17.5 %copy.90 = f32[8192,512]{1,0:T(8,128)} copy(f32[8192,512]{0,1:T(8,128)} %get-tuple-element.22) | data formatting | bytes 33554432 | tf_op jit(solution)/shard_map/reshape | solution.py:23
  84.9 14.9 %clamp_convert_fusion = bf16[16,2,256,512]{3,2,1,0:T(8,128)(2,1)} fusion(f32[16,2,256,512]{3,2,1,0:T(8,128)} %bitcast.75, f32[16,2,256,512]{3,2,1,0:T(8,128)} %div.30), kind=kLoop, calls=%fused_computation.3 | loop fusion | flops 12582912 | bytes 41943040 | tf_op jit(solution)/shard_map/convert_element_type | solution.py:26
  99.8 21.0 %copy.70 = bf16[16,2,256,512]{2,1,3,0:T(2,128)(2,1)} copy(bf16[16,2,256,512]{3,2,1,0:T(8,128)(2,1)} %clamp_convert_fusion) | data formatting | bytes 16777216 | tf_op jit(solution)/shard_map/convert_element_type | solution.py:26
  120.8 0.0 all-to-all-done.1
  120.8 6.0 %all-to-all-start = ((bf16[16,2,256,512]{2,1,3,0:T(2,128)(2,1)}), bf16[16,2,256,512]{2,1,3,0:T(2,128)(2,1)}, u32[]{:S(2)}, u32[]{:S(2)}) async-start(bf16[16,2,256,512]{2,1,3,0:T(2,128)(2,1)} %copy.70), calls=%async_computation | async-start | bytes 16777216 | tf_op jit(solution)/shard_map/all_to_all | solution.py:89
  126.9 0.0 all-gather.2.cloned.1.call-start
  126.9 0.7 all-gather.2.cloned.1.call-update
  127.6 0.0 reduce-scatter.2.cloned.1.call-start
  127.7 0.0 copy-done.4
  127.7 4.6 %all_gather.7 = bf16[8192,2]{0,1:T(2,128)(2,1)S(1)} all-gather(bf16[4096,2]{0,1:T(2,128)(2,1)S(1)} %convert_element_type.58), channel_id=1, replica_groups=mesh['outer'=16,'inner'=2] {'inner'}, dimensions={0}, use_global_device_ids=true | all-gather | bytes 49152 | tf_op jit(solution)/shard_map/all_gather | solution.py:73
  132.3 2.4 copy.59
  134.6 11.0 %mul.74 = f32[8192,2,256]{2,1,0:T(2,128)S(1)} broadcast(f32[8192,2]{1,0:T(8,128)} %copy.59), dimensions={0,1} | broadcast | bytes 16842752 | tf_op jit(solution)/shard_map/mul | solution.py:18
  145.6 7.2 %copy.94 = f32[1024,8,2,256]{3,1,2,0:T(8,128)} copy(f32[1024,8,2,256]{3,2,1,0:T(2,128)S(1)} %bitcast.73) | data formatting | bytes 33554432
  152.8 80.4 %all-gather.2.cloned.1.call-done = bf16[8192,512]{1,0:T(8,128)(2,1)} async-done(((bf16[4096,512]{1,0:T(8,128)(2,1)}), bf16[8192,512]{1,0:T(8,128)(2,1)}) %all-gather.2.cloned.1.call-update) | async-done | bytes 8388624 | tf_op jit(solution)/shard_map/all_gather | solution.py:72
  233.2 11.4 %fusion.9 = bf16[512,128]{1,0:T(8,128)(2,1)S(1)} fusion(bf16[128,8192]{1,0:T(8,128)(2,1)S(1)} %copy-done, f32[8192,512]{1,0:T(8,128)} %bitcast.74, bf16[8192,512]{1,0:T(8,128)(2,1)} %all-gather.2.cloned.1.call-done), kind=kOutput, calls=%fused_computation.21 | convolution fusion | flops 1086390272 | bytes 27394048 | tf_op jit(solution)/shard_map/dot_general | solution.py:78
  244.7 62.9 %all-to-all-done = bf16[16,2,256,512]{2,1,3,0:T(2,128)(2,1)} async-done(((bf16[16,2,256,512]{2,1,3,0:T(2,128)(2,1)}), bf16[16,2,256,512]{2,1,3,0:T(2,128)(2,1)}, u32[]{:S(2)}, u32[]{:S(2)}) %all-to-all-start) | async-done | bytes 8388640 | tf_op jit(solution)/shard_map/all_to_all | solution.py:89
  307.6 6.0 %mul.88 = f32[16,2,256,2,256]{2,1,4,3,0:T(2,128)} broadcast(bf16[16,2,256,2]{2,1,3,0:T(2,128)(2,1)S(1)} %all-to-all-done.1), dimensions={0,1,2,3} | broadcast | bytes 16809984 | tf_op jit(solution)/shard_map/mul | solution.py:18
  313.6 11.5 %multiply_reduce_fusion = bf16[2,256,512]{1,0,2:T(2,128)(2,1)S(1)} fusion(f32[16,2,256,512]{2,1,3,0:T(2,128)} %bitcast.76, bf16[16,2,256,512]{2,1,3,0:T(2,128)(2,1)} %all-to-all-done), kind=kLoop, calls=%fused_computation.2 | loop fusion | flops 12320768 | bytes 25690112 | tf_op jit(solution)/shard_map/reduce_sum | solution.py:94
  325.1 1.4 copy.73
  326.5 0.0 reduce-scatter.2.cloned.1.call-update
  326.5 0.0 copy-start.2
  326.6 2.6 fusion.2
  329.1 0.0 copy-done.2
  329.1 0.6 fusion.4
  329.7 1.4 multiply_convert_fusion.2
  331.1 2.3 copy.74
  333.4 1.7 fusion.7
  335.1 0.8 copy.75
  335.9 5.8 %reduce-scatter.2.cloned.1.call-done = bf16[1,256,512]{2,1,0:T(8,128)(2,1)} async-done(((bf16[2,256,512]{2,1,0:T(8,128)(2,1)}), bf16[1,256,512]{2,1,0:T(8,128)(2,1)}) %reduce-scatter.2.cloned.1.call-update) | async-done | bytes 262160 | tf_op jit(solution)/shard_map/reduce_scatter | solution.py:95
  341.7 1.8 bitcast_convert_fusion
  (5 shorter events, 0.1 us)
Async XLA Ops:
  7.2 8.9 %copy-start = (bf16[128,8192]{1,0:T(8,128)(2,1)S(1)}, bf16[128,8192]{1,0:T(8,128)(2,1)}, u32[]{:S(2)}) copy-start(bf16[128,8192]{1,0:T(8,128)(2,1)} %param.6) | copy-start | bytes 6291460
  7.2 1.8 copy-start.3
  9.0 4.8 %copy-start.1 = (bf16[128,4096]{0,1:T(8,128)(2,1)}, bf16[128,4096]{0,1:T(8,128)(2,1)S(1)}, u32[]{:S(2)}) copy-start(bf16[128,4096]{0,1:T(8,128)(2,1)S(1)} %copy.92) | copy-start | bytes 3145732
  25.0 95.9 %all-to-all-start.1 = ((bf16[16,2,256,2]{2,1,3,0:T(2,128)(2,1)}), bf16[16,2,256,2]{2,1,3,0:T(2,128)(2,1)S(1)}, u32[]{:S(2)}, u32[]{:S(2)}) async-start(bf16[16,2,256,2]{2,1,3,0:T(2,128)(2,1)} %copy.71), calls=%async_computation.1 | async-start | bytes 65536 | tf_op jit(solution)/shard_map/all_to_all | solution.py:90
  120.8 186.7 %all-to-all-start = ((bf16[16,2,256,512]{2,1,3,0:T(2,128)(2,1)}), bf16[16,2,256,512]{2,1,3,0:T(2,128)(2,1)}, u32[]{:S(2)}, u32[]{:S(2)}) async-start(bf16[16,2,256,512]{2,1,3,0:T(2,128)(2,1)} %copy.70), calls=%async_computation | async-start | bytes 16777216 | tf_op jit(solution)/shard_map/all_to_all | solution.py:89
  126.9 0.8 copy-start.4
  126.9 106.4 %all-gather.2.cloned.1.call-start = ((), (), s32[]{:S(2)}) async-start(), calls=%async_computation.3 | async-start | bytes 12582912 | tf_op jit(solution)/shard_map/all_gather | solution.py:72
  127.6 214.1 %reduce-scatter.2.cloned.1.call-start = ((), (), s32[]{:S(2)}) async-start(), calls=%async_computation.4 | async-start | bytes 786432 | tf_op jit(solution)/shard_map/reduce_scatter | solution.py:95
  326.5 2.6 copy-start.2
Sparse Core Ops, SparseCore 0:
  129.2 103.9 all-gather.1
  326.7 15.0 reduce-scatter.1
where the time goes:
time: 355 us; the launch traced here: 350 us
  waiting for transfers between devices  150 us (42%)
  local copies, waits for them, and re-layouts  111 us (31%)
  matrix products  29.7 us (8%)
  other arithmetic  28.9 us (8%)
  between operations  14.2 us (4%)
  starting transfers between devices  12.4 us (3%)
  blocking collectives  4.6 us (1%)
    all_gather x1, waiting for transfers between devices, on_device(): lax.all_gather(value_weight, 'inner', axis=0, tiled=True)  80.4 us
    all_to_all x1, waiting for transfers between devices, on_device(): lax.all_to_all(quant_grid, 'outer', split_axis=0, concat_axis=0, tiled=True)  62.9 us
    div x2, local copies, waits for them, and re-layouts, quantize(): scaled = jnp.clip(blocks / block_scale[..., None], -1.0, 1.0)  33.6 us
    convert_element_type x1, local copies, waits for them, and re-layouts, quantize(): quant = scaled.astype(jnp.bfloat16).reshape(gradient.shape)  21 us
    reshape x1, local copies, waits for them, and re-layouts, quantize(): blocks = gradient.reshape(leading + (-1, QUANT_BLOCK))  17.5 us
    mul x2, local copies, waits for them, and re-layouts, dequantize(): return (blocks * quant_scales[..., None]).reshape(leading + (-1,))  17 us
    convert_element_type x1, other arithmetic, quantize(): quant = scaled.astype(jnp.bfloat16).reshape(gradient.shape)  14.9 us
    reduce_sum x1, other arithmetic, on_device(): partial_sums = jnp.sum(dequantize(pieces[0], pieces[1]), axis=0)  11.5 us
  transfers between devices with their start and end apart: 4, of which 3 were waited for; matrix products, arithmetic and copies ran while one was open for 37% of the time, Pallas kernels for 0%

commit v1 on v0

v1 whole, which is shorter than its diff:
```python
import functools
import jax
import jax.numpy as jnp
from jax import lax
from jax.experimental import pallas as pl
from jax.experimental.pallas import tpu as pltpu
from jax.sharding import PartitionSpec as P

HEAD_DIM = 128
QUANT_BLOCK = 256
CLIP_RATIO = 1.5
Z_SPLIT = 4
F32 = jnp.float32
BF16 = jnp.bfloat16


def dot(a, b, ca=1, cb=0):
    return lax.dot_general(a, b, (((ca,), (cb,)), ((), ())), preferred_element_type=F32)


def body(dims, li, q_hbm, k_hbm, g_hbm, w_hbm, sc_ref, dq_out, dk_out, dw_out,
         q, k, g, w, xbuf, tbuf, vgbuf, probs, vals, vsend, vrecv, acc, pbuf, rbuf,
         loc_sem, own_sem, xs_sem, xr_sem, fs_sem, fr_sem, gxs_sem, gxr_sem, gfs_sem, gfr_sem,
         vs_sem, vr_sem, zs_sem, zr_sem):
    outer, inner, lo, runs, oc, kv_heads, group = dims
    o = lax.axis_index("outer")
    x = lax.axis_index("inner")
    z = o // lo
    l = o % lo
    part = outer * oc
    per = Z_SPLIT // runs
    width = per * oc
    count = q.shape[0]
    scale = HEAD_DIM ** -0.5

    def col(e, r):
        return pl.multiple_of(r * (outer // runs) * oc + ((l + e) % lo) * width, 128)

    def xdev(e):
        return (o, (x + e) % inner)

    def ldev(e):
        return (z * lo + (l + e) % lo, x)

    def remote(src, dst, ss, rs, dev):
        return pltpu.make_async_remote_copy(
            src_ref=src, dst_ref=dst, send_sem=ss, recv_sem=rs, device_id=dev,
            device_id_type=pl.DeviceIdType.MESH)

    q_cp = pltpu.make_async_copy(q_hbm, q, loc_sem.at[0])
    k_cp = pltpu.make_async_copy(k_hbm, k, loc_sem.at[1])
    g_cp = pltpu.make_async_copy(g_hbm, g, loc_sem.at[2])
    w_cp = pltpu.make_async_copy(w_hbm, w, loc_sem.at[3])
    order = [(r, e) for r in range(runs) for e in list(range(1, lo)) + [0]]
    order = [(r, e) for r in range(runs) for e in [lo // 2 + i for i in range(lo - lo // 2)]
             + [i for i in range(1, lo // 2)] + [0]] if lo > 1 else order

    def x_copy(ex, e, r):
        cols = pl.multiple_of(((x + ex) % inner) * part + col(e, r), 128)
        return remote(li.at[:, pl.ds(cols, width)], xbuf.at[inner - ex, e, r],
                      xs_sem.at[ex, e, r], xr_sem.at[inner - ex, e, r], xdev(ex))

    def own_copy(e, r):
        cols = pl.multiple_of(x * part + col(e, r), 128)
        return pltpu.make_async_copy(li.at[:, pl.ds(cols, width)], xbuf.at[0, e, r], own_sem.at[e, r])

    def fwd_own(e, r):
        cols = pl.multiple_of(x * part + col(e, r), 128)
        return remote(li.at[:, pl.ds(cols, width)], tbuf.at[lo - e, 0, r],
                      fs_sem.at[e, 0, r], fr_sem.at[lo - e, 0, r], ldev(e))

    def fwd(s, e, r):
        return remote(xbuf.at[s, e, r], tbuf.at[lo - e, s, r],
                      fs_sem.at[e, s, r], fr_sem.at[lo - e, s, r], ldev(e))

    q_cp.start()
    k_cp.start()
    for r, e in order:
        for ex in range(1, inner):
            x_copy(ex, e, r).start()
        if e:
            fwd_own(e, r).start()
    g_cp.start()
    for r, e in order:
        own_copy(e, r).start()
    w_cp.start()

    q_cp.wait()
    k_cp.wait()
    g_cp.wait()
    span = group * HEAD_DIM

    def heads(ref, h):
        return jnp.concatenate(
            [ref[:, (h * group + e) * HEAD_DIM:(h * group + e + 1) * HEAD_DIM] for e in range(group)], axis=0)

    key_pos = lax.broadcasted_iota(jnp.int32, (count, group * count), 0)
    query_pos = lax.broadcasted_iota(jnp.int32, (count, group * count), 1) % count
    admitted = key_pos <= query_pos
    for h in range(kv_heads):
        keys = k[:, h * HEAD_DIM:(h + 1) * HEAD_DIM]
        st = dot(keys, heads(q, h), 1, 1)
        st = jnp.where(admitted, st, -1e30)
        ex = jnp.exp((st - jnp.max(st, axis=0, keepdims=True)) * scale)
        p = ex * (1.0 / jnp.sum(ex, axis=0, keepdims=True))
        probs[h] = p
        vg = dot(p.astype(BF16), heads(g, h))
        vgbuf[0, 0, h * HEAD_DIM:(h + 1) * HEAD_DIM, :] = vg.T.astype(BF16)

    def vg_x(ex):
        return remote(vgbuf.at[0, 0], vgbuf.at[0, inner - ex], gxs_sem.at[ex], gxr_sem.at[inner - ex], xdev(ex))

    def vg_f(e, s):
        return remote(vgbuf.at[0, s], vgbuf.at[lo - e, s], gfs_sem.at[e, s], gfr_sem.at[lo - e, s], ldev(e))

    for ex in range(1, inner):
        vg_x(ex).start()
    for e in range(1, lo):
        vg_f(e, 0).start()

    w_cp.wait()
    first = True
    for r, e in order:
        own_copy(e, r).wait()
        for s in range(1, inner):
            x_copy(inner - s, e, r).wait_recv()
            if e:
                fwd(s, e, r).start()
        start = col(e, r)
        for j in range(vals.shape[-1] // QUANT_BLOCK):
            block = slice(j * QUANT_BLOCK, (j + 1) * QUANT_BLOCK)
            row_scale = sc_ref[j:j + 1, pl.ds(start, width)]
            lhs = jnp.concatenate(
                [(xbuf[s, e, r].astype(F32) * row_scale).astype(BF16) for s in range(inner)], axis=0)
            add = dot(lhs, w[pl.ds(start, width), block]).reshape(inner, count, QUANT_BLOCK)
            if first:
                vals[:, :, block] = add
            else:
                vals[:, :, block] += add
        first = False

    def val_copy(ex):
        return remote(vsend.at[ex], vrecv.at[inner - ex], vs_sem.at[ex], vr_sem.at[inner - ex], xdev(ex))

    for ex in range(1, inner):
        vsend[ex] = vals[ex].astype(BF16)
        val_copy(ex).start()
    for s in range(1, inner):
        vg_x(inner - s).wait_recv()
        for e in range(1, lo):
            vg_f(e, s).start()

    tile = min(width, 256)

    def add_term(vg_of, data_of, r, fresh):
        def step(c, carry):
            at = pl.multiple_of(c * tile, 128)
            data = data_of(at)
            for j in range(acc.shape[1] // QUANT_BLOCK):
                rows = slice(j * QUANT_BLOCK, (j + 1) * QUANT_BLOCK)
                term = dot(vg_of(rows), data)
                mean = jnp.sum(term * term, axis=0, keepdims=True) * (1.0 / QUANT_BLOCK)
                bound = CLIP_RATIO * jnp.sqrt(mean + 1e-6)
                kept = jnp.minimum(jnp.maximum(term, -bound), bound)
                if fresh:
                    acc[r, rows, pl.ds(at, tile)] = kept
                else:
                    acc[r, rows, pl.ds(at, tile)] += kept
            return carry
        lax.fori_loop(0, width // tile, step, 0)

    def owner(r, j):
        index = x * outer + r * (outer // runs) + l * per + j
        return index // inner, index % inner

    def z_copy(r, j):
        oo, xx = owner(r, j)
        n = r * per + j
        return remote(pbuf.at[n], rbuf.at[z], zs_sem.at[n], zr_sem.at[z], (oo, xx))

    def is_me(r, j):
        oo, xx = owner(r, j)
        return jnp.logical_and(oo == o, xx == x)

    def terms(r):
        for s in range(inner):
            add_term(lambda rows, s=s: vgbuf[0, s, rows, :],
                     lambda at, s=s: xbuf[s, 0, r, :, pl.ds(at, tile)], r, s == 0)
        for s in range(inner):
            def from_peer(d, carry, s=s):
                pltpu.make_async_copy(tbuf.at[d, s, r], tbuf.at[d, s, r], fr_sem.at[d, s, r]).wait()
                if r == 0:
                    pltpu.make_async_copy(vgbuf.at[d, s], vgbuf.at[d, s], gfr_sem.at[d, s]).wait()
                add_term(lambda rows: vgbuf[d, s, rows, :],
                         lambda at: tbuf[d, s, r, :, pl.ds(at, tile)], r, False)
                return carry
            lax.fori_loop(1, lo, from_peer, 0)
        summed = acc[r].T.astype(BF16)
        for j in range(per):
            n = r * per + j
            pbuf[n] = summed[j * oc:(j + 1) * oc]

            @pl.when(jnp.logical_not(is_me(r, j)))
            def _():
                z_copy(r, j).start()

            @pl.when(is_me(r, j))
            def _():
                pltpu.make_async_copy(pbuf.at[n], rbuf.at[z], zr_sem.at[z]).start()

    for r in range(runs):
        terms(r)

    for s in range(1, inner):
        val_copy(inner - s).wait_recv()
    total = vals[0]
    for s in range(1, inner):
        total = total + vrecv[s].astype(F32)
    values = total.astype(BF16)
    for h in range(kv_heads):
        cols = slice(h * HEAD_DIM, (h + 1) * HEAD_DIM)
        keys = k[:, cols]
        dp = dot(values[:, cols], heads(g, h), 1, 1)
        p = probs[h]
        delta = jnp.sum(p * dp, axis=0, keepdims=True)
        ds = p * (dp - delta)
        dk_out[:, cols] = (dot(ds.astype(BF16), heads(q, h)) * scale).astype(BF16)
        dq = (dot(ds.T.astype(BF16), keys) * scale).astype(BF16)
        for e in range(group):
            dq_out[:, (h * group + e) * HEAD_DIM:(h * group + e + 1) * HEAD_DIM] = dq[e * count:(e + 1) * count]

    for n in range(Z_SPLIT):
        pltpu.make_async_copy(rbuf.at[n], rbuf.at[n], zr_sem.at[n]).wait()
    out = rbuf[0].astype(F32)
    for n in range(1, Z_SPLIT):
        out = out + rbuf[n].astype(F32)
    dw_out[...] = out

    for ex in range(1, inner):
        vg_x(ex).wait_send()
        val_copy(ex).wait_send()
        for r, e in order:
            x_copy(ex, e, r).wait_send()
    for e in range(1, lo):
        for s in range(inner):
            vg_f(e, s).wait_send()
            for r in range(runs):
                (fwd(s, e, r) if s else fwd_own(e, r)).wait_send()
    for r in range(runs):
        for j in range(per):
            @pl.when(jnp.logical_not(is_me(r, j)))
            def _():
                z_copy(r, j).wait_send()


def on_device(layer_input, queries, key_states, output_grad, value_weight, value_scales):
    outer = lax.axis_size("outer")
    inner = lax.axis_size("inner")
    lo = outer // Z_SPLIT
    count, model = layer_input.shape
    kv = key_states.shape[1]
    oc = model // (outer * inner)
    runs = 2 if (2 * oc) % 128 == 0 else 1
    per = Z_SPLIT // runs
    width = per * oc
    kv_heads = kv // HEAD_DIM
    group = queries.shape[1] // kv
    dims = (outer, inner, lo, runs, oc, kv_heads, group)
    dma = pltpu.SemaphoreType.DMA
    anyspace = pl.BlockSpec(memory_space=pl.ANY)
    vmem = pl.BlockSpec(memory_space=pltpu.VMEM)
    return pl.pallas_call(
        functools.partial(body, dims),
        out_shape=(
            jax.ShapeDtypeStruct(queries.shape, BF16),
            jax.ShapeDtypeStruct(key_states.shape, BF16),
            jax.ShapeDtypeStruct((oc, kv), F32),
        ),
        in_specs=[anyspace] * 5 + [vmem],
        out_specs=(vmem, vmem, vmem),
        scratch_shapes=[
            pltpu.VMEM(queries.shape, BF16),
            pltpu.VMEM(key_states.shape, BF16),
            pltpu.VMEM(output_grad.shape, BF16),
            pltpu.VMEM(value_weight.shape, BF16),
            pltpu.VMEM((inner, lo, runs, count, width), BF16),
            pltpu.VMEM((lo, inner, runs, count, width), BF16),
            pltpu.VMEM((lo, inner, kv, count), BF16),
            pltpu.VMEM((kv_heads, count, group * count), F32),
            pltpu.VMEM((inner, count, kv), F32),
            pltpu.VMEM((inner, count, kv), BF16),
            pltpu.VMEM((inner, count, kv), BF16),
            pltpu.VMEM((runs, kv, width), F32),
            pltpu.VMEM((Z_SPLIT, oc, kv), BF16),
            pltpu.VMEM((Z_SPLIT, oc, kv), BF16),
            dma((4,)),
            dma((lo, runs)),
            dma((inner, lo, runs)),
            dma((inner, lo, runs)),
            dma((lo, inner, runs)),
            dma((lo, inner, runs)),
            dma((inner,)),
            dma((inner,)),
            dma((lo, inner)),
            dma((lo, inner)),
            dma((inner,)),
            dma((inner,)),
            dma((Z_SPLIT,)),
            dma((Z_SPLIT,)),
        ],
        compiler_params=pltpu.CompilerParams(
            has_side_effects=True, vmem_limit_bytes=50 * 1024 * 1024),
        cost_estimate=pl.CostEstimate(
            flops=4 * 1024 * 1024 * 1024, bytes_accessed=16 * 1024 * 1024, transcendentals=1024 * 1024),
    )(layer_input, queries, key_states, output_grad, value_weight, value_scales.T)


def solution(mesh):
    both = P(("outer", "inner"), None)
    return jax.shard_map(
        on_device, mesh=mesh,
        in_specs=(both, both, both, both, P("inner", None), P("inner", None)),
        out_specs=(both, both, both), check_vma=False)
```

time: 355 us -> 98.8 us (0.28)
  waiting for transfers between devices: 150 us -> 0 us
  local copies, waits for them, and re-layouts: 111 us -> 6.52 us
  Pallas kernels: 0 us -> 90.1 us
  matrix products: 29.7 us -> 0 us
  other arithmetic: 28.9 us -> 0 us
  between operations: 14.2 us -> 0.65 us
  starting transfers between devices: 12.4 us -> 0 us
  blocking collectives: 4.6 us -> 0 us
    pallas_call x0 -> x1, Pallas kernels: none -> 90.1 us  [on_device(): pl.pallas_call(functools.partial(body, dims), out_shape=(jax.ShapeDtypeSt...]
    all_gather x1 -> x0, waiting for transfers between devices: 80.4 us -> none  [on_device(): lax.all_gather(value_weight, 'inner', axis=0, tiled=True)]
    all_to_all x2 -> x0, waiting for transfers between devices: 62.9 us -> none  [the longest x1 62.9 us: on_device(): lax.all_to_all(quant_grid, 'outer', split_axis=0, concat_axis=0, tiled=True)]
    div x2 -> x0, local copies, waits for them, and re-layouts: 33.6 us -> none  [quantize(): scaled = jnp.clip(blocks / block_scale[..., None], -1.0, 1.0)]
    dot_general x6 -> x0, matrix products: 27.5 us -> none  [the longest x1 11.4 us: on_device(): jnp.dot(layer_input, weight_rows, preferred_element_type=jnp.float32)]
    convert_element_type x3 -> x0, local copies, waits for them, and re-layouts: 24.8 us -> none  [the longest x1 21 us: quantize(): quant = scaled.astype(jnp.bfloat16).reshape(gradient.shape)]
    reshape x5 -> x0, local copies, waits for them, and re-layouts: 21.9 us -> none  [the longest x1 17.5 us: quantize(): blocks = gradient.reshape(leading + (-1, QUANT_BLOCK))]
    mul x5 -> x0, local copies, waits for them, and re-layouts: 20.3 us -> none  [the longest x2 17 us: dequantize(): return (blocks * quant_scales[..., None]).reshape(leading + (-1,))]
  transfers between devices with their start and end apart: 4 -> 0, of which waited for: 3 -> 0; matrix products, arithmetic and copies ran while one was open for 37% -> 0% of each run, Pallas kernels for 0% -> 0%
where the time goes in v1:
time: 98.8 us; the launch traced here: 97.3 us
  Pallas kernels  90.1 us (91%)
  local copies, waits for them, and re-layouts  6.52 us (7%)
    pallas_call x1, Pallas kernels, on_device(): pl.pallas_call(functools.partial(body, dims), out_shape=(jax.ShapeDtypeSt...  90.1 us
    unnamed x11, local copies, waits for them, and re-layouts  6.52 us

profile of v1, /device:TPU:10, one launch (start us, length us, event | category | flops | bytes accessed | tf_op | source)
XLA Modules:
  0.0 97.3 jit_solution(16137474590722788443)
XLA Ops:
  0.6 0.0 copy-start
  0.6 1.2 %copy-done = bf16[128,4096]{1,0:T(8,128)(2,1)S(1)} copy-done((bf16[128,4096]{1,0:T(8,128)(2,1)S(1)}, bf16[128,4096]{1,0:T(8,128)(2,1)}, u32[]{:S(2)}) %copy-start) | copy-done | bytes 1048600
  1.9 0.0 copy-start.1
  1.9 1.2 %copy-done.1 = bf16[128,4096]{1,0:T(8,128)(2,1)S(1)} copy-done((bf16[128,4096]{1,0:T(8,128)(2,1)S(1)}, bf16[128,4096]{1,0:T(8,128)(2,1)}, u32[]{:S(2)}) %copy-start.1) | copy-done | bytes 1048600
  3.1 0.0 copy-start.2
  3.1 0.9 copy-done.2
  4.0 0.0 copy-start.3
  4.0 0.8 copy-done.3
  4.7 90.1 %shard_map.85 = (bf16[128,4096]{1,0:T(8,128)(2,1)S(1)}, bf16[128,512]{1,0:T(8,128)(2,1)S(1)}, f32[256,512]{1,0:T(8,128)S(1)}) custom-call(bf16[128,8192]{1,0:T(8,128)(2,1)} %li.1, bf16[128,4096]{1,0:T(8,128)(2,1)S(1)} %copy-done, bf16[128,512]{1,0:T(8,128)(2,1)S(1)} %copy-done.2, bf16[128,4096]{1,0:T(8,128)(2,1)S(1)} %copy-done.1, bf16[4096,512]{1,0:T(8,128)(2,1)} %w_hbm.1, ...), custom_call_target="tpu_custom_call" | custom-call | flops 4294967296 | bytes 16777216 | tf_op jit(solution)/shard_map/pallas_call | solution.py:272
  94.9 1.0 copy.12
  95.9 0.7 copy.13
  96.5 0.8 copy.14
Async XLA Ops:
  0.6 1.2 %copy-start = (bf16[128,4096]{1,0:T(8,128)(2,1)S(1)}, bf16[128,4096]{1,0:T(8,128)(2,1)}, u32[]{:S(2)}) copy-start(bf16[128,4096]{1,0:T(8,128)(2,1)} %q_hbm.1) | copy-start | bytes 3145732
  1.9 1.2 %copy-start.1 = (bf16[128,4096]{1,0:T(8,128)(2,1)S(1)}, bf16[128,4096]{1,0:T(8,128)(2,1)}, u32[]{:S(2)}) copy-start(bf16[128,4096]{1,0:T(8,128)(2,1)} %g_hbm.1) | copy-start | bytes 3145732
  3.1 0.9 copy-start.2
  4.0 0.8 copy-start.3

commit v2 on v1

v2 whole, which is shorter than its diff:
```python
import functools
import jax
import jax.numpy as jnp
from jax import lax
from jax.experimental import pallas as pl
from jax.experimental.pallas import tpu as pltpu
from jax.sharding import PartitionSpec as P

HEAD_DIM = 128
QUANT_BLOCK = 256
CLIP_RATIO = 1.5
Z_SPLIT = 4
F32 = jnp.float32
BF16 = jnp.bfloat16


def dot(a, b, ca=1, cb=0):
    return lax.dot_general(a, b, (((ca,), (cb,)), ((), ())), preferred_element_type=F32)


def body(dims, li, q_hbm, k_hbm, g_hbm, w_hbm, sc_ref, dq_hbm, dk_hbm, dw_out,
         q, k, g, w, xbuf, tbuf, vgbuf, probs, vals, vsend, vrecv, acc, pbuf, rbuf, dq_out, dk_out,
         loc_sem, own_sem, xs_sem, xr_sem, fs_sem, fr_sem, gxs_sem, gxr_sem, gfs_sem, gfr_sem,
         vs_sem, vr_sem, zs_sem, zr_sem, out_sem):
    outer, inner, lo, strips, sub, oc, kv_heads, group = dims
    o = lax.axis_index("outer")
    x = lax.axis_index("inner")
    z = o // lo
    l = o % lo
    pairs = lo // 2
    part = outer * oc
    runs = strips * sub
    per = Z_SPLIT // runs
    width = per * oc
    count = q.shape[0]
    scale = HEAD_DIM ** -0.5

    def peer(e):
        return ((l // 2 + e // 2) % pairs) * 2 + (l + e) % 2

    def back(e):
        return ((pairs - e // 2) % pairs) * 2 + e % 2

    def block_of(who, r):
        return (r // sub) * (outer // strips) + who * (Z_SPLIT // strips) + (r % sub) * per

    def col(e, r):
        return pl.multiple_of(block_of(peer(e), r) * oc, 128)

    def xdev(e):
        return (o, (x + e) % inner)

    def ldev(e):
        return (z * lo + peer(e), x)

    def remote(src, dst, ss, rs, dev):
        return pltpu.make_async_remote_copy(
            src_ref=src, dst_ref=dst, send_sem=ss, recv_sem=rs, device_id=dev,
            device_id_type=pl.DeviceIdType.MESH)

    q_cp = pltpu.make_async_copy(q_hbm, q, loc_sem.at[0])
    k_cp = pltpu.make_async_copy(k_hbm, k, loc_sem.at[1])
    g_cp = pltpu.make_async_copy(g_hbm, g, loc_sem.at[2])
    w_cp = pltpu.make_async_copy(w_hbm, w, loc_sem.at[3])
    order = list(range(2, lo)) + [1, 0]

    def x_copy(ex, e, r):
        cols = pl.multiple_of(((x + ex) % inner) * part + col(e, r), 128)
        return remote(li.at[:, pl.ds(cols, width)], xbuf.at[inner - ex, e, r],
                      xs_sem.at[ex, e, r], xr_sem.at[inner - ex, e, r], xdev(ex))

    def own_copy(e, r):
        cols = pl.multiple_of(x * part + col(e, r), 128)
        return pltpu.make_async_copy(li.at[:, pl.ds(cols, width)], xbuf.at[0, e, r], own_sem.at[e, r])

    def fwd_own(e, r):
        cols = pl.multiple_of(x * part + col(e, r), 128)
        return remote(li.at[:, pl.ds(cols, width)], tbuf.at[back(e), 0, r],
                      fs_sem.at[e, 0, r], fr_sem.at[back(e), 0, r], ldev(e))

    def fwd(s, e, r):
        return remote(xbuf.at[s, e, r], tbuf.at[back(e), s, r],
                      fs_sem.at[e, s, r], fr_sem.at[back(e), s, r], ldev(e))

    def issue(r):
        for e in order:
            for ex in range(1, inner):
                x_copy(ex, e, r).start()
            if e:
                fwd_own(e, r).start()

    k_cp.start()
    q_cp.start()
    issue(0)
    g_cp.start()
    for r in range(runs):
        for e in order:
            own_copy(e, r).start()
    w_cp.start()

    k_cp.wait()
    q_cp.wait()
    g_cp.wait()

    def heads(ref, h):
        return jnp.concatenate(
            [ref[:, (h * group + e) * HEAD_DIM:(h * group + e + 1) * HEAD_DIM] for e in range(group)], axis=0)

    key_pos = lax.broadcasted_iota(jnp.int32, (count, group * count), 0)
    query_pos = lax.broadcasted_iota(jnp.int32, (count, group * count), 1) % count
    admitted = key_pos <= query_pos
    for h in range(kv_heads):
        keys = k[:, h * HEAD_DIM:(h + 1) * HEAD_DIM]
        st = dot(keys, heads(q, h), 1, 1)
        st = jnp.where(admitted, st, -1e30)
        ex = jnp.exp((st - jnp.max(st, axis=0, keepdims=True)) * scale)
        p = ex * (1.0 / jnp.sum(ex, axis=0, keepdims=True))
        probs[h] = p
        vg = dot(p.astype(BF16), heads(g, h))
        vgbuf[0, 0, h * HEAD_DIM:(h + 1) * HEAD_DIM, :] = vg.T.astype(BF16)

    def vg_x(ex):
        return remote(vgbuf.at[0, 0], vgbuf.at[0, inner - ex], gxs_sem.at[ex], gxr_sem.at[inner - ex], xdev(ex))

    def vg_y(e, s):
        return remote(vgbuf.at[0, s], vgbuf.at[back(e), s], gfs_sem.at[e, s], gfr_sem.at[back(e), s], ldev(e))

    def vg_c(e, s):
        return remote(vgbuf.at[e, s], vgbuf.at[e + 1, s], gfs_sem.at[e + 1, s], gfr_sem.at[e + 1, s], ldev(1))

    chips = list(range(2, lo, 2))

    def share_vg(s):
        for e in chips:
            vg_y(e, s).start()
        vg_c(0, s).start()

    for ex in range(1, inner):
        vg_x(ex).start()
    share_vg(0)

    tile = min(width, 256)

    def add_term(vg_of, data_of, r, fresh):
        def step(c, carry):
            at = pl.multiple_of(c * tile, 128)
            data = data_of(at)
            for j in range(acc.shape[1] // QUANT_BLOCK):
                rows = slice(j * QUANT_BLOCK, (j + 1) * QUANT_BLOCK)
                term = dot(vg_of(rows), data)
                mean = jnp.sum(term * term, axis=0, keepdims=True) * (1.0 / QUANT_BLOCK)
                bound = CLIP_RATIO * jnp.sqrt(mean + 1e-6)
                kept = jnp.minimum(jnp.maximum(term, -bound), bound)
                if fresh:
                    acc[r, rows, pl.ds(at, tile)] = kept
                else:
                    acc[r, rows, pl.ds(at, tile)] += kept
            return carry
        lax.fori_loop(0, width // tile, step, 0)

    def terms(d, r):
        if d == 0:
            for s in range(inner):
                add_term(lambda rows, s=s: vgbuf[0, s, rows, :],
                         lambda at, s=s: xbuf[s, 0, r, :, pl.ds(at, tile)], r, s == 0)
            return

        for s in range(inner):
            arrived = pltpu.make_async_copy(tbuf.at[d, s, r], tbuf.at[d, s, r], fr_sem.at[d, s, r])
            arrived.wait()

        def one(s, carry):
            add_term(lambda rows: vgbuf[d, s, rows, :],
                     lambda at: tbuf[d, s, r, :, pl.ds(at, tile)], r, False)
            return carry
        lax.fori_loop(0, inner, one, 0)

    def owner(r, j):
        index = x * outer + block_of(l, r) + j
        return index // inner, index % inner

    def z_copy(r, j):
        oo, xx = owner(r, j)
        n = r * per + j
        return remote(pbuf.at[n], rbuf.at[z], zs_sem.at[n], zr_sem.at[z], (oo, xx))

    def is_me(r, j):
        oo, xx = owner(r, j)
        return jnp.logical_and(oo == o, xx == x)

    def deliver(r):
        summed = acc[r].T.astype(BF16)
        for j in range(per):
            n = r * per + j
            pbuf[n] = summed[j * oc:(j + 1) * oc]

            @pl.when(jnp.logical_not(is_me(r, j)))
            def _():
                z_copy(r, j).start()

            @pl.when(is_me(r, j))
            def _():
                pltpu.make_async_copy(pbuf.at[n], rbuf.at[z], zr_sem.at[z]).start()

    def val_copy(ex):
        return remote(vsend.at[ex], vrecv.at[inner - ex], vs_sem.at[ex], vr_sem.at[inner - ex], xdev(ex))

    def vg_arrived(e, s):
        pltpu.make_async_copy(vgbuf.at[e, s], vgbuf.at[e, s], gfr_sem.at[e, s]).wait()

    w_cp.wait()
    forward_order = [0] + list(range(1, lo))
    for r in range(runs):
        if r + 1 < runs:
            issue(r + 1)
        if r == 1 or runs == 1:
            for s in range(inner):
                for e in chips:
                    vg_arrived(e, s)
                    vg_c(e, s).start()
            for s in range(inner):
                for e in range(1, lo, 2):
                    vg_arrived(e, s)
        for i, e in enumerate(order):
            own_copy(e, r).wait()
            for s in range(1, inner):
                x_copy(inner - s, e, r).wait_recv()
                if e:
                    fwd(s, e, r).start()
            if r == 0 and i == 1:
                for s in range(1, inner):
                    vg_x(inner - s).wait_recv()
                    share_vg(s)
            start = col(e, r)
            for j in range(vals.shape[-1] // QUANT_BLOCK):
                block = slice(j * QUANT_BLOCK, (j + 1) * QUANT_BLOCK)
                row_scale = sc_ref[j:j + 1, pl.ds(start, width)]
                lhs = jnp.concatenate(
                    [(xbuf[s, e, r].astype(F32) * row_scale).astype(BF16) for s in range(inner)], axis=0)
                add = dot(lhs, w[pl.ds(start, width), block]).reshape(inner, count, QUANT_BLOCK)
                if r == 0 and i == 0:
                    vals[:, :, block] = add
                else:
                    vals[:, :, block] += add
            if r:
                terms(forward_order[i], r - 1)
        if r:
            deliver(r - 1)

    for ex in range(1, inner):
        vsend[ex] = vals[ex].astype(BF16)
        val_copy(ex).start()
    for d in forward_order:
        terms(d, runs - 1)
    deliver(runs - 1)

    for s in range(1, inner):
        val_copy(inner - s).wait_recv()
    total = vals[0]
    for s in range(1, inner):
        total = total + vrecv[s].astype(F32)
    values = total.astype(BF16)
    for h in range(kv_heads):
        cols = slice(h * HEAD_DIM, (h + 1) * HEAD_DIM)
        keys = k[:, cols]
        dp = dot(values[:, cols], heads(g, h), 1, 1)
        p = probs[h]
        delta = jnp.sum(p * dp, axis=0, keepdims=True)
        ds = p * (dp - delta)
        dk_out[:, cols] = (dot(ds.astype(BF16), heads(q, h)) * scale).astype(BF16)
        dq = (dot(ds.T.astype(BF16), keys) * scale).astype(BF16)
        for e in range(group):
            dq_out[:, (h * group + e) * HEAD_DIM:(h * group + e + 1) * HEAD_DIM] = dq[e * count:(e + 1) * count]
    dq_cp = pltpu.make_async_copy(dq_out, dq_hbm, out_sem.at[0])
    dk_cp = pltpu.make_async_copy(dk_out, dk_hbm, out_sem.at[1])
    dq_cp.start()
    dk_cp.start()

    for ex in range(1, inner):
        vg_x(ex).wait_send()
        val_copy(ex).wait_send()
        for r in range(runs):
            for e in order:
                x_copy(ex, e, r).wait_send()
    for s in range(inner):
        vg_c(0, s).wait_send()
        for e in chips:
            vg_y(e, s).wait_send()
            vg_c(e, s).wait_send()
        for e in range(1, lo):
            for r in range(runs):
                (fwd(s, e, r) if s else fwd_own(e, r)).wait_send()

    for n in range(Z_SPLIT):
        pltpu.make_async_copy(rbuf.at[n], rbuf.at[n], zr_sem.at[n]).wait()
    out = rbuf[0].astype(F32)
    for n in range(1, Z_SPLIT):
        out = out + rbuf[n].astype(F32)
    dw_out[...] = out
    for r in range(runs):
        for j in range(per):
            @pl.when(jnp.logical_not(is_me(r, j)))
            def _():
                z_copy(r, j).wait_send()
    dq_cp.wait()
    dk_cp.wait()


def on_device(layer_input, queries, key_states, output_grad, value_weight, value_scales):
    outer = lax.axis_size("outer")
    inner = lax.axis_size("inner")
    lo = outer // Z_SPLIT
    count, model = layer_input.shape
    kv = key_states.shape[1]
    oc = model // (outer * inner)
    strips = 2 if (2 * oc) % 128 == 0 else 1
    sub = 2 if oc % 128 == 0 else 1
    runs = strips * sub
    per = Z_SPLIT // runs
    width = per * oc
    kv_heads = kv // HEAD_DIM
    group = queries.shape[1] // kv
    dims = (outer, inner, lo, strips, sub, oc, kv_heads, group)
    dma = pltpu.SemaphoreType.DMA
    anyspace = pl.BlockSpec(memory_space=pl.ANY)
    vmem = pl.BlockSpec(memory_space=pltpu.VMEM)
    return pl.pallas_call(
        functools.partial(body, dims),
        out_shape=(
            jax.ShapeDtypeStruct(queries.shape, BF16),
            jax.ShapeDtypeStruct(key_states.shape, BF16),
            jax.ShapeDtypeStruct((oc, kv), F32),
        ),
        in_specs=[anyspace] * 5 + [vmem],
        out_specs=(anyspace, anyspace, vmem),
        scratch_shapes=[
            pltpu.VMEM(queries.shape, BF16),
            pltpu.VMEM(key_states.shape, BF16),
            pltpu.VMEM(output_grad.shape, BF16),
            pltpu.VMEM(value_weight.shape, BF16),
            pltpu.VMEM((inner, lo, runs, count, width), BF16),
            pltpu.VMEM((lo, inner, runs, count, width), BF16),
            pltpu.VMEM((lo, inner, kv, count), BF16),
            pltpu.VMEM((kv_heads, count, group * count), F32),
            pltpu.VMEM((inner, count, kv), F32),
            pltpu.VMEM((inner, count, kv), BF16),
            pltpu.VMEM((inner, count, kv), BF16),
            pltpu.VMEM((runs, kv, width), F32),
            pltpu.VMEM((Z_SPLIT, oc, kv), BF16),
            pltpu.VMEM((Z_SPLIT, oc, kv), BF16),
            pltpu.VMEM(queries.shape, BF16),
            pltpu.VMEM(key_states.shape, BF16),
            dma((4,)),
            dma((lo, runs)),
            dma((inner, lo, runs)),
            dma((inner, lo, runs)),
            dma((lo, inner, runs)),
            dma((lo, inner, runs)),
            dma((inner,)),
            dma((inner,)),
            dma((lo, inner)),
            dma((lo, inner)),
            dma((inner,)),
            dma((inner,)),
            dma((Z_SPLIT,)),
            dma((Z_SPLIT,)),
            dma((2,)),
        ],
        compiler_params=pltpu.CompilerParams(
            has_side_effects=True, vmem_limit_bytes=60 * 1024 * 1024),
        cost_estimate=pl.CostEstimate(
            flops=4 * 1024 * 1024 * 1024, bytes_accessed=16 * 1024 * 1024, transcendentals=1024 * 1024),
    )(layer_input, queries, key_states, output_grad, value_weight, value_scales.T)


def solution(mesh):
    both = P(("outer", "inner"), None)
    return jax.shard_map(
        on_device, mesh=mesh,
        in_specs=(both, both, both, both, P("inner", None), P("inner", None)),
        out_specs=(both, both, both), check_vma=False)
```

time: 98.8 us -> 86.8 us (0.88)
  Pallas kernels: 90.1 us -> 79 us
    pallas_call x1, Pallas kernels: 90.1 us -> 79 us  [on_device(): pl.pallas_call(functools.partial(body, dims), out_shape=(jax.ShapeDtypeSt...]
    unnamed x11 -> x3, local copies, waits for them, and re-layouts: 6.52 us -> 5.72 us
where the time goes in v2:
time: 86.8 us; the launch traced here: 85.3 us
  Pallas kernels  79 us (91%)
  local copies, waits for them, and re-layouts  5.72 us (7%)
    pallas_call x1, Pallas kernels, on_device(): pl.pallas_call(functools.partial(body, dims), out_shape=(jax.ShapeDtypeSt...  79 us
    unnamed x3, local copies, waits for them, and re-layouts  5.72 us

profile of v2, /device:TPU:10, one launch (start us, length us, event | category | flops | bytes accessed | tf_op | source)
XLA Modules:
  0.0 85.3 jit_solution(5804148206344628008)
XLA Ops:
  0.6 79.0 %shard_map.85 = (bf16[128,4096]{1,0:T(8,128)(2,1)}, bf16[128,512]{1,0:T(8,128)(2,1)}, f32[256,512]{1,0:T(8,128)}) custom-call(bf16[128,8192]{1,0:T(8,128)(2,1)} %li.1, bf16[128,4096]{1,0:T(8,128)(2,1)} %q_hbm.1, bf16[128,512]{1,0:T(8,128)(2,1)} %k_hbm.1, bf16[128,4096]{1,0:T(8,128)(2,1)} %g_hbm.1, bf16[4096,512]{1,0:T(8,128)(2,1)} %w_hbm.1, f32[2,4096]{1,0:T(2,128)} %bitcast.1), custom_call_target="tpu_custom_call" | custom-call | flops 4294967296 | bytes 16777216 | tf_op jit(solution)/shard_map/pallas_call | solution.py:327
  79.6 2.3 %copy.12 = bf16[128,4096]{1,0:T(8,128)(2,1)} copy(bf16[128,4096]{1,0:T(8,128)(2,1)} %get-tuple-element.6) | data formatting | bytes 2097152
  81.9 1.6 %copy.13 = bf16[128,512]{1,0:T(8,128)(2,1)} copy(bf16[128,512]{1,0:T(8,128)(2,1)} %get-tuple-element.7) | data formatting | bytes 262144
  83.4 1.9 %copy.14 = f32[256,512]{1,0:T(8,128)} copy(f32[256,512]{1,0:T(8,128)} %get-tuple-element.8) | data formatting | bytes 1048576

commit v3 on v2

--- a/solution.py
+++ b/solution.py
@@ -21,7 +21,7 @@
 def body(dims, li, q_hbm, k_hbm, g_hbm, w_hbm, sc_ref, dq_hbm, dk_hbm, dw_out,
          q, k, g, w, xbuf, tbuf, vgbuf, probs, vals, vsend, vrecv, acc, pbuf, rbuf, dq_out, dk_out,
          loc_sem, own_sem, xs_sem, xr_sem, fs_sem, fr_sem, gxs_sem, gxr_sem, gfs_sem, gfr_sem,
-         vs_sem, vr_sem, zs_sem, zr_sem, out_sem):
+         vs_sem, vr_sem, zs_sem, zr_sem, out_sem, hops, hr_sem, hs_sem):
     outer, inner, lo, strips, sub, oc, kv_heads, group = dims
     o = lax.axis_index("outer")
     x = lax.axis_index("inner")
@@ -34,6 +34,7 @@
     width = per * oc
     count = q.shape[0]
     scale = HEAD_DIM ** -0.5
+    hop = inner == 2 and sub == 2
 
     def peer(e):
         return ((l // 2 + e // 2) % pairs) * 2 + (l + e) % 2
@@ -41,11 +42,14 @@
     def back(e):
         return ((pairs - e // 2) % pairs) * 2 + e % 2
 
-    def block_of(who, r):
-        return (r // sub) * (outer // strips) + who * (Z_SPLIT // strips) + (r % sub) * per
-
-    def col(e, r):
-        return pl.multiple_of(block_of(peer(e), r) * oc, 128)
+    def block_of(who, r, at):
+        low = (r % sub + 1 + at) % 2 if hop else r % sub
+        strip = r // sub
+        strip = strip + (at // (inner // 2)) * (strips - 1 - 2 * strip)
+        return strip * (outer // strips) + who * (Z_SPLIT // strips) + low * per
+
+    def col(e, r, at):
+        return pl.multiple_of(block_of(peer(e), r, at) * oc, 128)
 
     def xdev(e):
         return (o, (x + e) % inner)
@@ -65,16 +69,17 @@
     order = list(range(2, lo)) + [1, 0]
 
     def x_copy(ex, e, r):
-        cols = pl.multiple_of(((x + ex) % inner) * part + col(e, r), 128)
+        to = (x + ex) % inner
+        cols = pl.multiple_of(to * part + col(e, r, to), 128)
         return remote(li.at[:, pl.ds(cols, width)], xbuf.at[inner - ex, e, r],
                       xs_sem.at[ex, e, r], xr_sem.at[inner - ex, e, r], xdev(ex))
 
     def own_copy(e, r):
-        cols = pl.multiple_of(x * part + col(e, r), 128)
+        cols = pl.multiple_of(x * part + col(e, r, x), 128)
         return pltpu.make_async_copy(li.at[:, pl.ds(cols, width)], xbuf.at[0, e, r], own_sem.at[e, r])
 
     def fwd_own(e, r):
-        cols = pl.multiple_of(x * part + col(e, r), 128)
+        cols = pl.multiple_of(x * part + col(e, r, x), 128)
         return remote(li.at[:, pl.ds(cols, width)], tbuf.at[back(e), 0, r],
                       fs_sem.at[e, 0, r], fr_sem.at[back(e), 0, r], ldev(e))
 
@@ -176,7 +181,7 @@
         lax.fori_loop(0, inner, one, 0)
 
     def owner(r, j):
-        index = x * outer + block_of(l, r) + j
+        index = x * outer + block_of(l, r, x) + j
         return index // inner, index % inner
 
     def z_copy(r, j):
@@ -187,12 +192,34 @@
     def is_me(r, j):
         oo, xx = owner(r, j)
         return jnp.logical_and(oo == o, xx == x)
+
+    def cross(r):
+        return remote(pbuf.at[r], hops.at[r // 2], zs_sem.at[r], hr_sem.at[r // 2], xdev(1))
+
+    def onward(r):
+        oo = ((1 - x) * outer + block_of(l, r, 1 - x)) // inner
+        return oo, remote(hops.at[r // 2], rbuf.at[z], hs_sem.at[r // 2], zr_sem.at[z], (oo, x))
+
+    def pass_on(r):
+        cross(r).wait_recv()
+        oo, copy = onward(r)
+
+        @pl.when(oo != o)
+        def _():
+            copy.start()
+
+        @pl.when(oo == o)
+        def _():
+            pltpu.make_async_copy(hops.at[r // 2], rbuf.at[z], zr_sem.at[z]).start()
 
     def deliver(r):
         summed = acc[r].T.astype(BF16)
         for j in range(per):
             n = r * per + j
             pbuf[n] = summed[j * oc:(j + 1) * oc]
+            if hop and r % 2 == 0:
+                cross(r).start()
+                continue
 
             @pl.when(jnp.logical_not(is_me(r, j)))
             def _():
@@ -201,6 +228,8 @@
             @pl.when(is_me(r, j))
             def _():
                 pltpu.make_async_copy(pbuf.at[n], rbuf.at[z], zr_sem.at[z]).start()
+        if hop and r % 2 == 1:
+            pass_on(r - 1)
 
     def val_copy(ex):
         return remote(vsend.at[ex], vrecv.at[inner - ex], vs_sem.at[ex], vr_sem.at[inner - ex], xdev(ex))
@@ -231,7 +260,7 @@
                 for s in range(1, inner):
                     vg_x(inner - s).wait_recv()
                     share_vg(s)
-            start = col(e, r)
+            start = col(e, r, x)
             for j in range(vals.shape[-1] // QUANT_BLOCK):
                 block = slice(j * QUANT_BLOCK, (j + 1) * QUANT_BLOCK)
                 row_scale = sc_ref[j:j + 1, pl.ds(start, width)]
@@ -298,6 +327,14 @@
         out = out + rbuf[n].astype(F32)
     dw_out[...] = out
     for r in range(runs):
+        if hop and r % 2 == 0:
+            cross(r).wait_send()
+            oo, copy = onward(r)
+
+            @pl.when(oo != o)
+            def _():
+                copy.wait_send()
+            continue
         for j in range(per):
             @pl.when(jnp.logical_not(is_me(r, j)))
             def _():
@@ -365,6 +402,9 @@
             dma((Z_SPLIT,)),
             dma((Z_SPLIT,)),
             dma((2,)),
+            pltpu.VMEM((2, oc, kv), BF16),
+            dma((2,)),
+            dma((2,)),
         ],
         compiler_params=pltpu.CompilerParams(
             has_side_effects=True, vmem_limit_bytes=60 * 1024 * 1024),

time: 86.8 us -> 73.2 us (0.84); the launches traced: 85.3 us -> 72.9 us
  Pallas kernels: 79 us -> 66.5 us
    pallas_call x1, Pallas kernels: 79 us -> 66.5 us  [on_device(): pl.pallas_call(functools.partial(body, dims), out_shape=(jax.ShapeDtypeSt...]
where the time goes in v3:
time: 73.2 us; the launch traced here: 72.9 us
  Pallas kernels  66.5 us (91%)
  local copies, waits for them, and re-layouts  5.72 us (8%)
    pallas_call x1, Pallas kernels, on_device(): pl.pallas_call(functools.partial(body, dims), out_shape=(jax.ShapeDtypeSt...  66.5 us
    unnamed x3, local copies, waits for them, and re-layouts  5.72 us

profile of v3, /device:TPU:10, one launch (start us, length us, event | category | flops | bytes accessed | tf_op | source)
XLA Modules:
  0.0 72.9 jit_solution(2825722005165214947)
XLA Ops:
  0.6 66.5 %shard_map.85 = (bf16[128,4096]{1,0:T(8,128)(2,1)}, bf16[128,512]{1,0:T(8,128)(2,1)}, f32[256,512]{1,0:T(8,128)}) custom-call(bf16[128,8192]{1,0:T(8,128)(2,1)} %li.1, bf16[128,4096]{1,0:T(8,128)(2,1)} %q_hbm.1, bf16[128,512]{1,0:T(8,128)(2,1)} %k_hbm.1, bf16[128,4096]{1,0:T(8,128)(2,1)} %g_hbm.1, bf16[4096,512]{1,0:T(8,128)(2,1)} %w_hbm.1, f32[2,4096]{1,0:T(2,128)} %bitcast.1), custom_call_target="tpu_custom_call" | custom-call | flops 4294967296 | bytes 16777216 | tf_op jit(solution)/shard_map/pallas_call | solution.py:364
  67.2 2.3 %copy.12 = bf16[128,4096]{1,0:T(8,128)(2,1)} copy(bf16[128,4096]{1,0:T(8,128)(2,1)} %get-tuple-element.6) | data formatting | bytes 2097152
  69.5 1.6 %copy.13 = bf16[128,512]{1,0:T(8,128)(2,1)} copy(bf16[128,512]{1,0:T(8,128)(2,1)} %get-tuple-element.7) | data formatting | bytes 262144
  71.0 1.9 %copy.14 = f32[256,512]{1,0:T(8,128)} copy(f32[256,512]{1,0:T(8,128)} %get-tuple-element.8) | data formatting | bytes 1048576
